TPU v7x, 32 devices: a whole 2x2x4 slice. The times are simulated.
32 devices in a mesh: groups: 2 (over x), sector: 8 (over z, y), op: 2 (over core).
Axes of the slice: x: 2, y: 2, z: 4, core: 2. Of those that a mesh axis runs over, the one named last changes fastest.
Arguments:
- wavefunction: bfloat16 [48, 256, 256], P(('groups', 'sector')), parts along dimension 0, may hold values from -18 to 18
- left_ops: bfloat16 [32, 48, 256, 256], P('op', ('groups', 'sector')), parts along dimension 1, may hold values from -0.375 to 0.375
- right_ops: bfloat16 [32, 48, 256, 256], P('op', ('groups', 'sector')), parts along dimension 1, may hold values from -0.125 to 0.125
- energy: float32 [48], P(('groups', 'sector')), parts along dimension 0, may hold values from 0.5 to 4
- term_class: int32 [32], P('op'), may hold values from 0 to 4
- target_sector: int32 [48, 5], P('groups'), parts along dimension 0, may hold values from 0 to 23, as said below
Outputs:
- sigma: bfloat16 [48, 256, 256], P(('groups', 'sector'), 'op'), parts along dimension 0
- residual: bfloat16 [48, 256, 256], P(('groups', 'sector'), 'op'), parts along dimension 0
There are 2 independent parts, one for each index of `groups`. A program takes and returns all parts, laid end to end along the dimension named above; an argument that names none is the same for every part. Nothing has to cross between parts.
Inputs may be any that keep to these rules, and one draw needn't show every extreme that they name: target_sector[s, c] is a sector of the index (s // 3 + o) mod 8 of sector, with o = 0, 1, -1, 2, -2 for c = 0, 1, 2, 3, 4; target_sector[s, 0] = s.
All inputs are finite; a program needn't handle non-finite values.
Results may differ from a plain program's by a relative error of at most 0.0045.
Values sent between devices are 32-bit elements; how exact they have to be, the bound alone decides.
A program may use at most 128 MiB of HBM per device.

v0:
```python
import jax
import jax.numpy as jnp
from jax import lax
from jax.sharding import PartitionSpec as P


def passed_along(block, axis, distance):
    devices = range(lax.axis_size(axis))
    route = [((i - distance) % len(devices), i) for i in devices]
    return lax.ppermute(block, axis, route)


def local(wavefunction, left_ops, right_ops, energy, term_class, target_sector):
    cycle_size = lax.axis_size("sector")
    my_index = lax.axis_index("sector")
    sec_local = wavefunction.shape[0]
    block_size = wavefunction.shape[1]
    class_count = target_sector.shape[1]
    offsets = [0, 1, -1, 2, -2]
    halves = jnp.einsum(
        "ksij,sjl->ksil", left_ops, wavefunction, preferred_element_type=jnp.float32
    ).astype(jnp.bfloat16)
    term_blocks = jnp.einsum(
        "ksil,ksml->ksim", halves, right_ops, preferred_element_type=jnp.float32
    )
    selector = (term_class[:, None] == jnp.arange(class_count, dtype=jnp.int32)[None, :]).astype(
        jnp.float32
    )
    grouped = jnp.einsum("kc,ksim->csim", selector, term_blocks, precision=lax.Precision.HIGHEST)
    accrued = jnp.zeros(grouped.shape[1:], jnp.float32)
    for column in range(class_count):
        offset = offsets[column]
        piece = grouped[column]
        if offset != 0:
            piece = passed_along(piece, "sector", offset)
        source_dev = (my_index - offset) % cycle_size
        target_ids = lax.dynamic_slice_in_dim(target_sector, source_dev * sec_local, sec_local, 0)[
            :, column
        ]
        slot_index = target_ids - my_index * sec_local
        chooser = (jnp.arange(sec_local, dtype=jnp.int32)[:, None] == slot_index[None, :]).astype(
            jnp.float32
        )
        accrued = accrued + jnp.einsum(
            "tj,jim->tim", chooser, piece, precision=lax.Precision.HIGHEST
        )
    accrued = lax.psum_scatter(accrued, "op", scatter_dimension=1, tiled=True)
    share = block_size // lax.axis_size("op")
    own_rows = lax.dynamic_slice_in_dim(
        wavefunction, lax.axis_index("op") * share, share, 1
    ).astype(jnp.float32)
    sigma_full = accrued + energy[:, None, None] * own_rows
    projection, squared_norm = lax.psum(
        (jnp.sum(own_rows * sigma_full), jnp.sum(own_rows * own_rows)), ("sector", "op")
    )
    quotient = projection / squared_norm
    return (
        sigma_full.astype(jnp.bfloat16),
        (sigma_full - quotient * own_rows).astype(jnp.bfloat16),
    )


def solution(mesh):
    in_specs = (
        P(("groups", "sector"), None, None),
        P("op", ("groups", "sector"), None, None),
        P("op", ("groups", "sector"), None, None),
        P(("groups", "sector")),
        P("op"),
        P("groups", None),
    )
    out_specs = (P(("groups", "sector"), "op", None), P(("groups", "sector"), "op", None))
    return jax.shard_map(local, mesh=mesh, in_specs=in_specs, out_specs=out_specs, check_vma=False)
```

profile of v0, /device:TPU:0, one launch (start us, length us, event | category | flops | bytes accessed | tf_op | source)
XLA Modules:
  0.0 185.7 jit_solution(8305143918427797429)
XLA Ops:
  7.2 0.0 copy-start
  7.2 0.0 all-reduce.4.cloned.1.call-start
  7.2 0.9 copy-done
  8.2 4.6 %fusion.5 = bf16[3,256,16,256]{3,1,2,0:T(8,128)(2,1)S(1)} fusion(bf16[16,3,256,256]{3,2,1,0:T(8,128)(2,1)} %param.7, bf16[3,256,256]{2,1,0:T(8,128)(2,1)S(1)} %copy-done), kind=kOutput, calls=%fused_computation.6 | convolution fusion | flops 1610612736 | bytes 12976128 | tf_op jit(solution)/shard_map/ksij,sjl->ksil/dot_general | solution.py:20
  12.8 6.3 %copy.71 = bf16[3,256,16,256]{3,2,1,0:T(8,128)(2,1)} copy(bf16[3,256,16,256]{3,1,2,0:T(8,128)(2,1)S(1)} %fusion.5) | data formatting | bytes 12582912 | tf_op jit(solution)/shard_map/ksij,sjl->ksil/dot_general | solution.py:20
  19.1 0.0 copy-start.3
  19.1 13.6 %fusion.3 = f32[16,3,256,256]{3,2,1,0:T(8,128)} fusion(bf16[16,3,256,256]{3,2,1,0:T(8,128)(2,1)} %param.8, bf16[16,3,256,256]{2,0,3,1:T(8,128)(2,1)} %bitcast.55), kind=kOutput, calls=%fused_computation.4 | convolution fusion | flops 1610612736 | bytes 25165824 | tf_op jit(solution)/shard_map/ksil,ksml->ksim/dot_general | solution.py:23
  32.7 0.0 copy-done.3
  32.7 15.8 %fusion = f32[5,3,256,256]{3,0,2,1:T(8,128)S(1)} fusion(f32[16,3,256,256]{3,2,1,0:T(8,128)} %fusion.3, s32[16]{0:T(128)S(1)} %copy-done.3), kind=kOutput, calls=%fused_computation | convolution fusion | flops 188743760 | bytes 16515136 | tf_op jit(solution)/shard_map/kc,ksim->csim/dot_general | solution.py:29
  48.5 0.0 copy-start.1
  48.5 3.4 %fusion.43 = (f32[1,3,256,256]{3,0,2,1:T(1,128)S(1)}, f32[1,3,256,256]{3,0,2,1:T(1,128)S(1)}, f32[1,3,256,256]{3,0,2,1:T(1,128)S(1)}, f32[1,3,256,256]{3,0,2,1:T(1,128)S(1)}, f32[1,3,256,256]{3,0,2,1:T(1,128)S(1)}) fusion(f32[5,3,256,256]{3,0,2,1:T(8,128)S(1)} %fusion), kind=kLoop, calls=%fused_computation.65 | loop fusion | bytes 7864320 | tf_op jit(solution)/shard_map/slice | solution.py:33
  52.0 0.9 copy.75
  52.9 3.0 %collective-permute-start = (f32[3,256,256]{2,1,0:T(8,128)}, f32[3,256,256]{2,1,0:T(8,128)S(1)}, u32[]{:S(2)}, u32[]{:S(2)}) collective-permute-start(f32[3,256,256]{2,1,0:T(8,128)} %bitcast.54), channel_id=1, source_target_pairs={{14,0},{0,2},{2,4},{4,6},{6,8},{8,10},{10,12},{12,14},{15,1},{1,3}... | collective-permute-start | bytes 2359304 | tf_op jit(solution)/shard_map/ppermute | solution.py:10
  55.9 0.9 copy.73
  56.8 1.6 collective-permute-start.2
  58.4 0.9 copy.72
  59.3 2.2 %collective-permute-start.3 = (f32[3,256,256]{2,1,0:T(8,128)}, f32[3,256,256]{2,1,0:T(8,128)S(1)}, u32[]{:S(2)}, u32[]{:S(2)}) collective-permute-start(f32[3,256,256]{2,1,0:T(8,128)} %bitcast.51), channel_id=1, source_target_pairs={{4,0},{6,2},{8,4},{10,6},{12,8},{14,10},{0,12},{2,14},{5,1},{7,3},... | collective-permute-start | bytes 2359304 | tf_op jit(solution)/shard_map/ppermute | solution.py:10
  61.6 0.9 copy.74
  62.5 1.2 collective-permute-start.1
  63.7 0.0 copy-done.1
  63.7 0.1 constant_dynamic-slice_fusion.3
  63.8 1.4 fusion.9
  65.3 14.0 %collective-permute-done.2 = f32[3,256,256]{2,1,0:T(8,128)S(1)} collective-permute-done((f32[3,256,256]{2,1,0:T(8,128)}, f32[3,256,256]{2,1,0:T(8,128)S(1)}, u32[]{:S(2)}, u32[]{:S(2)}) %collective-permute-start.2) | collective-permute-done | bytes 786464 | tf_op jit(solution)/shard_map/ppermute | solution.py:10
  79.3 1.4 fusion.14
  80.7 0.0 copy-start.4
  80.7 0.0 copy-start.2
  80.7 14.1 %collective-permute-done.3 = f32[3,256,256]{2,1,0:T(8,128)S(1)} collective-permute-done((f32[3,256,256]{2,1,0:T(8,128)}, f32[3,256,256]{2,1,0:T(8,128)S(1)}, u32[]{:S(2)}, u32[]{:S(2)}) %collective-permute-start.3) | collective-permute-done | bytes 786464 | tf_op jit(solution)/shard_map/ppermute | solution.py:10
  94.8 1.4 fusion.12
  96.2 0.0 collective-permute-done
  96.2 1.6 convolution_add_fusion.1
  97.8 11.2 %collective-permute-done.1 = f32[3,256,256]{2,1,0:T(8,128)} collective-permute-done((f32[3,256,256]{2,1,0:T(8,128)}, f32[3,256,256]{2,1,0:T(8,128)}, u32[]{:S(2)}, u32[]{:S(2)}) %collective-permute-start.1) | collective-permute-done | bytes 786464 | tf_op jit(solution)/shard_map/ppermute | solution.py:10
  109.0 4.0 %fusion.8 = f32[3,256,256]{2,0,1:T(4,128)} fusion(f32[3,256,256]{2,0,1:T(4,128)S(1)} %fusion.12, f32[3,256,256]{2,0,1:T(4,128)S(1)} %fusion.14, f32[3,256,256]{2,0,1:T(4,128)S(1)} %convolution_add_fusion.1, f32[3,256,256]{2,1,0:T(8,128)} %collective-permute-done.1, s32[3]{0:T(128)S(1)} %get-tuple-element.24), kind=kOutput, calls=%fused_computation.10 | convolution fusion | flops 7667721 | bytes 3932172 | tf_op jit(solution)/shard_map/tj,jim->tim/dot_general | solution.py:44
  112.9 0.0 all-reduce.4.cloned.1.call-update
  113.0 0.0 copy-done.4
  113.0 0.6 dynamic-slice
  114.2 23.9 %all-reduce.4.cloned.1.call-done = f32[3,256,256]{2,0,1:T(4,128)} async-done(((f32[3,256,256]{2,0,1:T(4,128)}), f32[3,256,256]{2,0,1:T(4,128)}) %all-reduce.4.cloned.1.call-update) | async-done | bytes 786448
  138.2 0.0 copy-done.2
  138.2 2.0 %fusion.20 = (f32[]{:T(128)}, f32[]{:T(128)}) fusion(bf16[3,128,256]{2,1,0:T(8,128)(2,1)S(1)} %constant_dynamic-slice_fusion, f32[3]{0:T(128)S(1)} %copy-done.2, f32[3,256,256]{2,0,1:T(4,128)} %all-reduce.4.cloned.1.call-done, u32[]{:T(128)S(6)} %multiply.1), kind=kLoop, calls=%fused_computation.31 | loop fusion | flops 688126 | bytes 589848 | tf_op jit(solution)/shard_map/reduce_sum | solution.py:54
  140.2 34.5 %all-reduce.1 = (f32[]{:T(128)}, f32[]{:T(128)}) all-reduce(f32[]{:T(128)} %get-tuple-element.7, f32[]{:T(128)} %get-tuple-element.6), channel_id=1, replica_groups=mesh['groups'=2,'sector'=8,'op'=2] {'sector','op'}, use_global_device_ids=true, to_apply=%region_2.3 | all-reduce | flops 2 | bytes 16 | tf_op jit(solution)/shard_map/psum | solution.py:53
  176.0 1.4 fusion.22
  177.4 0.7 copy.22
  178.1 0.7 copy.23
  (4 shorter events, 0.0 us)
Async XLA Ops:
  7.2 1.0 copy-start
  7.2 131.0 %all-reduce.4.cloned.1.call-start = ((), (), s32[]{:S(2)}) async-start(), calls=%async_computation | async-start | bytes 2097152
  19.1 13.6 %copy-start.3 = (s32[16]{0:T(128)S(1)}, s32[16]{0:T(128)}, u32[]{:S(2)}) copy-start(s32[16]{0:T(128)} %param.10) | copy-start | bytes 196
  48.5 15.2 %copy-start.1 = (s32[24,5]{0,1:T(8,128)S(1)}, s32[24,5]{0,1:T(8,128)}, u32[]{:S(2)}) copy-start(s32[24,5]{0,1:T(8,128)} %param.11) | copy-start | bytes 1444
  52.9 43.3 %collective-permute-start = (f32[3,256,256]{2,1,0:T(8,128)}, f32[3,256,256]{2,1,0:T(8,128)S(1)}, u32[]{:S(2)}, u32[]{:S(2)}) collective-permute-start(f32[3,256,256]{2,1,0:T(8,128)} %bitcast.54), channel_id=1, source_target_pairs={{14,0},{0,2},{2,4},{4,6},{6,8},{8,10},{10,12},{12,14},{15,1},{1,3}... | collective-permute-start | bytes 2359304 | tf_op jit(solution)/shard_map/ppermute | solution.py:10
  56.8 22.5 %collective-permute-start.2 = (f32[3,256,256]{2,1,0:T(8,128)}, f32[3,256,256]{2,1,0:T(8,128)S(1)}, u32[]{:S(2)}, u32[]{:S(2)}) collective-permute-start(f32[3,256,256]{2,1,0:T(8,128)} %bitcast.52), channel_id=1, source_target_pairs={{12,0},{14,2},{0,4},{2,6},{4,8},{6,10},{8,12},{10,14},{13,1},{15,3... | collective-permute-start | bytes 2359304 | tf_op jit(solution)/shard_map/ppermute | solution.py:10
  59.3 35.5 %collective-permute-start.3 = (f32[3,256,256]{2,1,0:T(8,128)}, f32[3,256,256]{2,1,0:T(8,128)S(1)}, u32[]{:S(2)}, u32[]{:S(2)}) collective-permute-start(f32[3,256,256]{2,1,0:T(8,128)} %bitcast.51), channel_id=1, source_target_pairs={{4,0},{6,2},{8,4},{10,6},{12,8},{14,10},{0,12},{2,14},{5,1},{7,3},... | collective-permute-start | bytes 2359304 | tf_op jit(solution)/shard_map/ppermute | solution.py:10
  62.5 46.5 %collective-permute-start.1 = (f32[3,256,256]{2,1,0:T(8,128)}, f32[3,256,256]{2,1,0:T(8,128)}, u32[]{:S(2)}, u32[]{:S(2)}) collective-permute-start(f32[3,256,256]{2,1,0:T(8,128)} %bitcast.53), channel_id=1, source_target_pairs={{2,0},{4,2},{6,4},{8,6},{10,8},{12,10},{14,12},{0,14},{3,1},{5,3},... | collective-permute-start | bytes 2359304 | tf_op jit(solution)/shard_map/ppermute | solution.py:10
  80.7 32.2 %copy-start.4 = (u32[32]{0:T(128)S(1)}, u32[32]{0:T(128)}, u32[]{:S(2)}) copy-start(u32[32]{0:T(128)} %constant.66) | copy-start | bytes 388
  80.7 57.5 %copy-start.2 = (f32[3]{0:T(128)S(1)}, f32[3]{0:T(128)}, u32[]{:S(2)}) copy-start(f32[3]{0:T(128)} %param.9) | copy-start | bytes 40
Sparse Core Ops, SparseCore 0:
  113.1 25.0 all-reduce.3
where the time goes:
time: 186 us
  waiting for transfers between devices  63.3 us (34%)
  matrix products  43.8 us (24%)
  blocking collectives  34.5 us (19%)
  local copies, waits for them, and re-layouts  16.5 us (9%)
  between operations  16.2 us (9%)
  starting transfers between devices  8.07 us (4%)
  other arithmetic  3.41 us (2%)
    ppermute x4, waiting for transfers between devices, passed_along(): return lax.ppermute(block, axis, route)  39.3 us
    psum x1, blocking collectives, local(): lax.psum((jnp.sum(own_rows * sigma_full), jnp.sum(own_rows * own_rows)),...  34.5 us
    unnamed x2, waiting for transfers between devices  24 us
    dot_general x1, matrix products, local(): jnp.einsum('kc,ksim->csim', selector, term_blocks, precision=lax.Precisio...  15.8 us
    dot_general x1, matrix products, local(): jnp.einsum('ksil,ksml->ksim', halves, right_ops, preferred_element_type=j...  13.6 us
    dot_general x5, matrix products, local(): jnp.einsum('tj,jim->tim', chooser, piece, precision=lax.Precision.HIGHEST)  9.72 us
    ppermute x4, starting transfers between devices, passed_along(): return lax.ppermute(block, axis, route)  8.04 us
    unnamed x17, local copies, waits for them, and re-layouts  6.7 us
  transfers between devices with their start and end apart: 5, of which 4 were waited for; matrix products, arithmetic and copies ran while one was open for 5% of the time, Pallas kernels for 0%

commit v1 on v0

v1 whole, which is shorter than its diff:
```python
import functools

import jax
import jax.numpy as jnp
from jax import lax
from jax.experimental import pallas as pl
from jax.experimental.pallas import tpu as pltpu
from jax.sharding import PartitionSpec as P

MESH = pl.DeviceIdType.MESH
GROUP = 4
OWN, TO_PEER, VIA_PEER, JOINED, ALONE = range(5)


def kernel(n, n_op, tc, ts, energy, w_ref, left, right, sigma_out, resid_out,
           lbuf, rbuf, acc, sib, tot, peer_in, via_in, alone_in, joined_in, joined, sig, scal,
           lsem, rsem, sib_s, sib_r, peer_s, peer_r, via_s, via_r, alone_s, alone_r, join_s, join_r, scal_s, scal_r):
    me = lax.axis_index("sector")
    core = lax.axis_index("op")
    other = 1 - core
    odd = lax.rem(me, 2)
    sign = 1 - 2 * odd
    peer = me + sign
    ahead = lax.rem(me + 2 * sign + n, n)
    behind = lax.rem(me - 2 * sign + n, n)
    terms, nsec = left.shape[0], left.shape[1]
    block = left.shape[2]
    rows = block // n_op
    groups = terms // GROUP
    everyone = n * n_op
    flat = me * n_op + core

    def loads(s, g):
        part = pl.ds(g * GROUP, GROUP)
        return (
            pltpu.make_async_copy(left.at[part, s], lbuf.at[s, part], lsem.at[s, g]),
            pltpu.make_async_copy(right.at[part, s], rbuf.at[s, part], rsem.at[s, g]),
        )

    for s in range(nsec):
        for g in range(groups):
            for copy in loads(s, g):
                copy.start()

    barrier = pltpu.get_barrier_semaphore()

    def greet(i, carry):
        dev = lax.rem(flat + i, everyone)
        pl.semaphore_signal(barrier, inc=1, device_id={"sector": dev // n_op, "op": lax.rem(dev, n_op)},
                            device_id_type=MESH)
        return carry

    lax.fori_loop(1, everyone, greet, 0)

    role_class = (0, 1 + odd, 2 - odd, 3 + odd, 4 - odd)

    def remote(src, dst, send, recv, where):
        return pltpu.make_async_remote_copy(src_ref=src, dst_ref=dst, send_sem=send, recv_sem=recv,
                                            device_id=where, device_id_type=MESH)

    def sib_copy(s):
        return remote(acc.at[s, other], sib.at[s], sib_s.at[s], sib_r.at[s], {"op": other})

    def via_copy(s):
        return remote(tot.at[s, VIA_PEER], via_in.at[s], via_s.at[s], via_r.at[s], {"sector": peer})

    def peer_copy(s):
        return remote(tot.at[s, TO_PEER], peer_in.at[s], peer_s.at[s], peer_r.at[s], {"sector": peer})

    def alone_copy(s):
        return remote(tot.at[s, ALONE], alone_in.at[s], alone_s.at[s], alone_r.at[s], {"sector": behind})

    def joined_copy(s):
        return remote(joined.at[s], joined_in.at[s], join_s.at[s], join_r.at[s], {"sector": ahead})

    def compute(s):
        acc[s] = jnp.zeros(acc.shape[1:], jnp.float32)

        def step(g, carry):
            for copy in loads(s, g):
                copy.wait()
            lhs = lbuf[s, pl.ds(g * GROUP, GROUP)].reshape(GROUP * block, block)
            half = jnp.dot(lhs, w_ref[s], preferred_element_type=jnp.float32).astype(jnp.bfloat16)
            products = [
                lax.dot_general(half[i * block:(i + 1) * block], rbuf[s, g * GROUP + i],
                                (((1,), (1,)), ((), ())), preferred_element_type=jnp.float32)
                for i in range(GROUP)
            ]
            for h in range(n_op):
                for r in range(5):
                    total = acc[s, h, r]
                    for i in range(GROUP):
                        chosen = jnp.where(tc[g * GROUP + i] == role_class[r], 1.0, 0.0)
                        total = total + chosen * products[i][h * rows:(h + 1) * rows]
                    acc[s, h, r] = total
            return carry

        lax.fori_loop(0, groups, step, 0)

    def finish(s):
        sib_copy(s).wait_recv()
        for r in (VIA_PEER, ALONE, TO_PEER, JOINED, OWN):
            tot[s, r] = acc[s, core, r] + sib[s, r]
            if r == VIA_PEER:
                via_copy(s).start()
            if r == ALONE:
                alone_copy(s).start()

    for s in range(nsec):
        compute(s)
        if s == 0:
            pl.semaphore_wait(barrier, everyone - 1)
        sib_copy(s).start()
        if s > 0:
            finish(s - 1)
    finish(nsec - 1)
    for s in range(nsec):
        peer_copy(s).start()

    def weights(source, class_id, dest):
        return [
            [jnp.where(ts[source * nsec + j, class_id] == dest * nsec + t, 1.0, 0.0) for j in range(nsec)]
            for t in range(nsec)
        ]

    own_w = weights(me, 3 + odd, ahead)
    via_w = weights(peer, 1 + odd, ahead)
    for s in range(nsec):
        via_copy(s).wait_recv()
    for t in range(nsec):
        total = own_w[t][0] * tot[0, JOINED] + via_w[t][0] * via_in[0]
        for j in range(1, nsec):
            total = total + own_w[t][j] * tot[j, JOINED] + via_w[t][j] * via_in[j]
        joined[t] = total
        joined_copy(t).start()

    mine = pl.ds(pl.multiple_of(core * rows, rows), rows)
    norm = jnp.zeros((8, 128), jnp.float32)
    proj = jnp.zeros((8, 128), jnp.float32)

    def fold(x):
        y = x.reshape(rows // 8, 8, block).sum(axis=0)
        z = y[:, 0:128]
        for c in range(1, block // 128):
            z = z + y[:, c * 128:(c + 1) * 128]
        return z

    for t in range(nsec):
        amp = w_ref[t, mine, :].astype(jnp.float32)
        norm = norm + fold(amp * amp)
        sig[t] = energy[t] * amp + tot[t, OWN]
    alone_w = weights(ahead, 4 - odd, me)
    for s in range(nsec):
        alone_copy(s).wait_recv()
    for t in range(nsec):
        total = sig[t]
        for j in range(nsec):
            total = total + alone_w[t][j] * alone_in[j]
        sig[t] = total
    peer_w = weights(peer, 2 - odd, me)
    for s in range(nsec):
        peer_copy(s).wait_recv()
    for t in range(nsec):
        total = sig[t]
        for j in range(nsec):
            total = total + peer_w[t][j] * peer_in[j]
        sig[t] = total
    for t in range(nsec):
        joined_copy(t).wait_recv()
        total = sig[t] + joined_in[t]
        sig[t] = total
        proj = proj + fold(w_ref[t, mine, :].astype(jnp.float32) * total)
    scal[0, 0] = proj
    scal[0, 1] = norm

    def scal_copy(i):
        dev = lax.rem(flat + i, everyone)
        return remote(scal.at[0], scal.at[i], scal_s.at[i], scal_r.at[i],
                      {"sector": dev // n_op, "op": lax.rem(dev, n_op)})

    def scal_start(i, carry):
        scal_copy(i).start()
        return carry

    def scal_recv(i, carry):
        scal_copy(i).wait_recv()
        return carry

    def scal_sent(i, carry):
        scal_copy(i).wait_send()
        return carry

    lax.fori_loop(1, everyone, scal_start, 0)
    for t in range(nsec):
        sigma_out[t] = sig[t].astype(jnp.bfloat16)
        sib_copy(t).wait_send()
        via_copy(t).wait_send()
        peer_copy(t).wait_send()
        alone_copy(t).wait_send()
        joined_copy(t).wait_send()
    lax.fori_loop(1, everyone, scal_recv, 0)
    sums = scal[...].sum(axis=0)
    theta = jnp.sum(sums[0], keepdims=True) / jnp.sum(sums[1], keepdims=True)
    for t in range(nsec):
        resid_out[t] = (sig[t] - theta * w_ref[t, mine, :].astype(jnp.float32)).astype(jnp.bfloat16)
    lax.fori_loop(1, everyone, scal_sent, 0)


def local(n, n_op, wavefunction, left_ops, right_ops, energy, term_class, target_sector):
    terms, nsec, block, _ = left_ops.shape
    rows = block // n_op
    vmem = pl.BlockSpec(memory_space=pltpu.VMEM)
    smem = pl.BlockSpec(memory_space=pltpu.SMEM)
    hbm = pl.BlockSpec(memory_space=pl.ANY)
    out = jax.ShapeDtypeStruct((nsec, rows, block), jnp.bfloat16)
    f32 = jnp.float32
    piece = (nsec, rows, block)
    pairs = []
    for _ in range(5):
        pairs += [pltpu.SemaphoreType.DMA((nsec,)), pltpu.SemaphoreType.DMA((nsec,))]
    return pl.pallas_call(
        functools.partial(kernel, n, n_op),
        out_shape=(out, out),
        in_specs=[smem, smem, smem, vmem, hbm, hbm],
        out_specs=(vmem, vmem),
        scratch_shapes=[
            pltpu.VMEM((nsec, terms, block, block), jnp.bfloat16),
            pltpu.VMEM((nsec, terms, block, block), jnp.bfloat16),
            pltpu.VMEM((nsec, n_op, 5, rows, block), f32),
            pltpu.VMEM((nsec, 5, rows, block), f32),
            pltpu.VMEM((nsec, 5, rows, block), f32),
            pltpu.VMEM(piece, f32),
            pltpu.VMEM(piece, f32),
            pltpu.VMEM(piece, f32),
            pltpu.VMEM(piece, f32),
            pltpu.VMEM(piece, f32),
            pltpu.VMEM(piece, f32),
            pltpu.VMEM((n * n_op, 2, 8, 128), f32),
            pltpu.SemaphoreType.DMA((nsec, terms // GROUP)),
            pltpu.SemaphoreType.DMA((nsec, terms // GROUP)),
            *pairs,
            pltpu.SemaphoreType.DMA((n * n_op,)),
            pltpu.SemaphoreType.DMA((n * n_op,)),
        ],
        compiler_params=pltpu.CompilerParams(
            collective_id=0, has_side_effects=True, vmem_limit_bytes=48 * 1024 * 1024
        ),
        cost_estimate=pl.CostEstimate(
            flops=4 * terms * nsec * block**3, bytes_accessed=4 * terms * nsec * block**2, transcendentals=0
        ),
    )(term_class, target_sector, energy, wavefunction, left_ops, right_ops)


def solution(mesh):
    in_specs = (
        P(("groups", "sector"), None, None),
        P("op", ("groups", "sector"), None, None),
        P("op", ("groups", "sector"), None, None),
        P(("groups", "sector")),
        P("op"),
        P("groups", None),
    )
    out_specs = (P(("groups", "sector"), "op", None), P(("groups", "sector"), "op", None))
    body = functools.partial(local, mesh.shape["sector"], mesh.shape["op"])
    return jax.shard_map(body, mesh=mesh, in_specs=in_specs, out_specs=out_specs, check_vma=False)
```

time: 186 us -> 41.7 us (0.22)
  waiting for transfers between devices: 63.3 us -> 0 us
  matrix products: 43.8 us -> 0 us
  Pallas kernels: 0 us -> 36.4 us
  blocking collectives: 34.5 us -> 0 us
  between operations: 16.2 us -> 0.64 us
  local copies, waits for them, and re-layouts: 16.5 us -> 4.43 us
  starting transfers between devices: 8.07 us -> 0 us
  other arithmetic: 3.41 us -> 0 us
    dot_general x8 -> x0, matrix products: 43.8 us -> none  [the longest x1 15.8 us: local(): jnp.einsum('kc,ksim->csim', selector, term_blocks, precision=lax.Precisio...]
    ppermute x4 -> x0, waiting for transfers between devices: 39.3 us -> none  [passed_along(): return lax.ppermute(block, axis, route)]
    pallas_call x0 -> x1, Pallas kernels: none -> 36.4 us  [local(): pl.pallas_call(functools.partial(kernel, n, n_op), out_shape=(out, out),...]
    psum x1 -> x0, blocking collectives: 34.5 us -> none  [local(): lax.psum((jnp.sum(own_rows * sigma_full), jnp.sum(own_rows * own_rows)),...]
    unnamed x2 -> x0, waiting for transfers between devices: 24 us -> none
    ppermute x4 -> x0, starting transfers between devices: 8.04 us -> none  [passed_along(): return lax.ppermute(block, axis, route)]
    dot_general x1 -> x0, local copies, waits for them, and re-layouts: 6.28 us -> none  [local(): jnp.einsum('ksij,sjl->ksil', left_ops, wavefunction, preferred_element_ty...]
    slice x1 -> x0, local copies, waits for them, and re-layouts: 3.44 us -> none  [local(): piece = grouped[column]]
  transfers between devices with their start and end apart: 5 -> 0, of which waited for: 4 -> 0; matrix products, arithmetic and copies ran while one was open for 5% -> 0% of each run, Pallas kernels for 0% -> 0%
where the time goes in v1:
time: 41.7 us; the launch traced here: 41.5 us
  Pallas kernels  36.4 us (87%)
  local copies, waits for them, and re-layouts  4.43 us (11%)
  between operations  0.64 us (2%)
    pallas_call x1, Pallas kernels, local(): pl.pallas_call(functools.partial(kernel, n, n_op), out_shape=(out, out),...  36.4 us
    unnamed x9, local copies, waits for them, and re-layouts  4.43 us

profile of v1, /device:TPU:0, one launch (start us, length us, event | category | flops | bytes accessed | tf_op | source)
XLA Modules:
  0.0 41.5 jit_solution(2148388932679174472)
XLA Ops:
  0.6 0.8 %copy.8.ts = s32[24,5]{1,0:T(8,128)S(1)} copy(s32[24,5]{0,1:T(8,128)} %param.11) | data formatting | bytes 960 | tf_op args[5]
  1.4 0.0 copy-start
  1.4 1.0 %copy-done = bf16[3,256,256]{2,1,0:T(8,128)(2,1)S(1)} copy-done((bf16[3,256,256]{2,1,0:T(8,128)(2,1)S(1)}, bf16[3,256,256]{2,1,0:T(8,128)(2,1)}, u32[]{:S(2)}) %copy-start) | copy-done | bytes 393240
  2.4 0.0 copy-start.1
  2.4 0.7 %copy-done.1 = s32[16]{0:T(128)S(1)} copy-done((s32[16]{0:T(128)S(1)}, s32[16]{0:T(128)}, u32[]{:S(2)}) %copy-start.1) | copy-done | bytes 88
  3.0 0.0 copy-start.2
  3.0 0.7 %copy-done.2 = f32[3]{0:T(128)S(1)} copy-done((f32[3]{0:T(128)S(1)}, f32[3]{0:T(128)}, u32[]{:S(2)}) %copy-start.2) | copy-done | bytes 36
  3.7 36.4 %shard_map.77 = (bf16[3,128,256]{2,1,0:T(8,128)(2,1)S(1)}, bf16[3,128,256]{2,1,0:T(8,128)(2,1)S(1)}) custom-call(s32[16]{0:T(128)S(1)} %copy-done.1, s32[24,5]{1,0:T(8,128)S(1)} %copy.8.ts, f32[3]{0:T(128)S(1)} %copy-done.2, bf16[3,256,256]{2,1,0:T(8,128)(2,1)S(1)} %copy-done, bf16[16,3,256,256]{3,2,1,0:T(8,128)(2,1)} %left.1, bf16[16,3,256,256]{3,2,1,0:T(8,128)(2,1)} %right.1), custom_call_target="tpu_custom_call" | custom-call | flops 3221225472 | bytes 12582912 | tf_op jit(solution)/shard_map/pallas_call | solution.py:221
  40.1 0.7 %copy.11 = bf16[3,128,256]{2,1,0:T(8,128)(2,1)} copy(bf16[3,128,256]{2,1,0:T(8,128)(2,1)S(1)} %get-tuple-element.4) | data formatting | bytes 393216
  40.8 0.7 %copy.12 = bf16[3,128,256]{2,1,0:T(8,128)(2,1)} copy(bf16[3,128,256]{2,1,0:T(8,128)(2,1)S(1)} %get-tuple-element.5) | data formatting | bytes 393216
Async XLA Ops:
  1.4 1.0 %copy-start = (bf16[3,256,256]{2,1,0:T(8,128)(2,1)S(1)}, bf16[3,256,256]{2,1,0:T(8,128)(2,1)}, u32[]{:S(2)}) copy-start(bf16[3,256,256]{2,1,0:T(8,128)(2,1)} %w_ref.1) | copy-start | bytes 1179652
  2.4 0.7 %copy-start.1 = (s32[16]{0:T(128)S(1)}, s32[16]{0:T(128)}, u32[]{:S(2)}) copy-start(s32[16]{0:T(128)} %tc.1) | copy-start | bytes 196
  3.0 0.7 %copy-start.2 = (f32[3]{0:T(128)S(1)}, f32[3]{0:T(128)}, u32[]{:S(2)}) copy-start(f32[3]{0:T(128)} %energy.1) | copy-start | bytes 40

commit v2 on v1

v2 whole, which is shorter than its diff:
```python
import functools

import jax
import jax.numpy as jnp
from jax import lax
from jax.experimental import pallas as pl
from jax.experimental.pallas import tpu as pltpu
from jax.sharding import PartitionSpec as P

MESH = pl.DeviceIdType.MESH
GROUP = 4
ALONE, VIA_PEER, TO_PEER, JOINED, OWN = range(5)
FIRST = 2
PARTS = 2


def kernel(n, n_op, tc_in, ts_in, energy_in, w_in, left, right, sigma_out, resid_out,
           tc, ts, energy, w_ref, lbuf, rbuf, acc, sib, tot, peer_in, via_in, alone_in, joined_in, joined, sig, scal,
           small, lsem, rsem, sib_s, sib_r, peer_s, peer_r, via_s, via_r, alone_s, alone_r, join_s, join_r, scal_s, scal_r):
    me = lax.axis_index("sector")
    core = lax.axis_index("op")
    other = 1 - core
    odd = lax.rem(me, 2)
    sign = 1 - 2 * odd
    peer = me + sign
    ahead = lax.rem(me + 2 * sign + n, n)
    behind = lax.rem(me - 2 * sign + n, n)
    terms, nsec = left.shape[0], left.shape[1]
    block = left.shape[2]
    rows = block // n_op
    groups = terms // GROUP
    everyone = n * n_op
    flat = me * n_op + core

    def loads(s, g):
        part = pl.ds(g * GROUP, GROUP)
        return (
            pltpu.make_async_copy(left.at[part, s], lbuf.at[s, part], lsem.at[s, g]),
            pltpu.make_async_copy(right.at[part, s], rbuf.at[s, part], rsem.at[s, g]),
        )

    smalls = [
        pltpu.make_async_copy(src, dst, small.at[i])
        for i, (src, dst) in enumerate(((w_in, w_ref), (tc_in, tc), (ts_in, ts), (energy_in, energy)))
    ]
    for copy in smalls:
        copy.start()
    for s in range(nsec):
        for g in range(groups):
            for copy in loads(s, g):
                copy.start()

    barrier = pltpu.get_barrier_semaphore()

    def greet(i, carry):
        dev = lax.rem(flat + i, everyone)
        pl.semaphore_signal(barrier, inc=1, device_id={"sector": dev // n_op, "op": lax.rem(dev, n_op)},
                            device_id_type=MESH)
        return carry

    lax.fori_loop(1, everyone, greet, 0)

    role_class = (4 - odd, 2 - odd, 1 + odd, 3 + odd, 0)

    def remote(src, dst, send, recv, where):
        return pltpu.make_async_remote_copy(src_ref=src, dst_ref=dst, send_sem=send, recv_sem=recv,
                                            device_id=where, device_id_type=MESH)

    part_rows = rows // PARTS

    def sib_copy(s, b):
        roles = pl.ds(0, FIRST) if b == 0 else pl.ds(FIRST, 5 - FIRST)
        return remote(acc.at[s, other, roles], sib.at[s, roles], sib_s.at[s, b], sib_r.at[s, b], {"op": other})

    def via_copy(s, p):
        part = pl.ds(p * part_rows, part_rows)
        return remote(tot.at[s, VIA_PEER, part], via_in.at[s, part], via_s.at[s, p], via_r.at[s, p], {"sector": peer})

    def peer_copy(s):
        return remote(tot.at[s, TO_PEER], peer_in.at[s], peer_s.at[s], peer_r.at[s], {"sector": peer})

    def alone_copy(s):
        return remote(tot.at[s, ALONE], alone_in.at[s], alone_s.at[s], alone_r.at[s], {"sector": behind})

    def joined_copy(s, p):
        part = pl.ds(p * part_rows, part_rows)
        return remote(joined.at[s, part], joined_in.at[s, part], join_s.at[s, p], join_r.at[s, p], {"sector": ahead})

    def compute(s, g):
        for copy in loads(s, g):
            copy.wait()
        lhs = lbuf[s, pl.ds(g * GROUP, GROUP)].reshape(GROUP * block, block)
        half = jnp.dot(lhs, w_ref[s], preferred_element_type=jnp.float32).astype(jnp.bfloat16)
        products = [
            lax.dot_general(half[i * block:(i + 1) * block], rbuf[s, g * GROUP + i],
                            (((1,), (1,)), ((), ())), preferred_element_type=jnp.float32)
            for i in range(GROUP)
        ]
        chosen = [[jnp.where(tc[g * GROUP + i] == c, 1.0, 0.0) for i in range(GROUP)] for c in role_class]
        for h in range(n_op):
            for r in range(5):
                total = chosen[r][0] * products[0][h * rows:(h + 1) * rows]
                for i in range(1, GROUP):
                    total = total + chosen[r][i] * products[i][h * rows:(h + 1) * rows]
                acc[s, h, r] = total if g == 0 else acc[s, h, r] + total

    def finish_first(s):
        sib_copy(s, 0).wait_recv()
        tot[s, ALONE] = acc[s, core, ALONE] + sib[s, ALONE]
        alone_copy(s).start()
        tot[s, VIA_PEER] = acc[s, core, VIA_PEER] + sib[s, VIA_PEER]
        via_copy(s, 0).start()
        if s == 0:
            via_copy(s, 1).start()
        if s == nsec - 1:
            for q in range(1, nsec):
                via_copy(q, 1).start()

    def finish_second(s):
        sib_copy(s, 1).wait_recv()
        for r in (TO_PEER, JOINED, OWN):
            tot[s, r] = acc[s, core, r] + sib[s, r]
        if s == nsec - 1:
            for q in range(nsec):
                peer_copy(q).start()

    for copy in smalls:
        copy.wait()
    for s in range(nsec):
        for g in range(groups):
            compute(s, g)
            if s > 0 and g == 0:
                finish_first(s - 1)
            if s > 0 and g == groups - 1:
                finish_second(s - 1)
        if s == 0:
            pl.semaphore_wait(barrier, everyone - 1)
        for b in range(2):
            sib_copy(s, b).start()
    finish_first(nsec - 1)
    finish_second(nsec - 1)

    def weights(source, class_id, dest):
        return [
            [jnp.where(ts[class_id, source * nsec + j] == dest * nsec + t, 1.0, 0.0) for j in range(nsec)]
            for t in range(nsec)
        ]

    own_w = weights(me, 3 + odd, ahead)
    via_w = weights(peer, 1 + odd, ahead)
    for p in range(PARTS):
        part = pl.ds(p * part_rows, part_rows)
        for s in range(nsec):
            via_copy(s, p).wait_recv()
        for t in range(nsec):
            total = own_w[t][0] * tot[0, JOINED, part] + via_w[t][0] * via_in[0, part]
            for j in range(1, nsec):
                total = total + own_w[t][j] * tot[j, JOINED, part] + via_w[t][j] * via_in[j, part]
            joined[t, part] = total
            joined_copy(t, p).start()

    mine = pl.ds(pl.multiple_of(core * rows, rows), rows)
    norm = jnp.zeros((8, block), jnp.float32)
    proj = jnp.zeros((8, block), jnp.float32)

    def fold(x):
        return x.reshape(x.shape[0] // 8, 8, block).sum(axis=0)

    def narrow(x):
        y = jnp.sum(x, axis=0, keepdims=True)
        z = y[:, 0:128]
        for c in range(1, block // 128):
            z = z + y[:, c * 128:(c + 1) * 128]
        return z

    for t in range(nsec):
        amp = w_ref[t, mine, :].astype(jnp.float32)
        norm = norm + fold(amp * amp)
        sig[t] = energy[t] * amp + tot[t, OWN]
    scal[0, 1:2] = narrow(norm)
    alone_w = weights(ahead, 4 - odd, me)
    for s in range(nsec):
        alone_copy(s).wait_recv()
    for t in range(nsec):
        total = sig[t]
        for j in range(nsec):
            total = total + alone_w[t][j] * alone_in[j]
        sig[t] = total
    peer_w = weights(peer, 2 - odd, me)
    for s in range(nsec):
        peer_copy(s).wait_recv()
    for t in range(nsec):
        total = sig[t]
        for j in range(nsec):
            total = total + peer_w[t][j] * peer_in[j]
        sig[t] = total
    for p in range(PARTS):
        part = pl.ds(p * part_rows, part_rows)
        here = pl.ds(pl.multiple_of(core * rows + p * part_rows, part_rows), part_rows)
        for t in range(nsec):
            joined_copy(t, p).wait_recv()
            total = sig[t, part] + joined_in[t, part]
            sig[t, part] = total
            proj = proj + fold(w_ref[t, here, :].astype(jnp.float32) * total)
    scal[0, 0:1] = narrow(proj)

    def scal_copy(i):
        dev = lax.rem(flat + i, everyone)
        return remote(scal.at[0], scal.at[i], scal_s.at[i], scal_r.at[i],
                      {"sector": dev // n_op, "op": lax.rem(dev, n_op)})

    def scal_start(i, carry):
        scal_copy(i).start()
        return carry

    def scal_recv(i, carry):
        scal_copy(i).wait_recv()
        return carry

    def scal_sent(i, carry):
        scal_copy(i).wait_send()
        return carry

    lax.fori_loop(1, everyone, scal_start, 0)
    for t in range(nsec):
        sigma_out[t] = sig[t].astype(jnp.bfloat16)
        for p in range(2):
            sib_copy(t, p).wait_send()
        for p in range(PARTS):
            via_copy(t, p).wait_send()
            joined_copy(t, p).wait_send()
        peer_copy(t).wait_send()
        alone_copy(t).wait_send()
    lax.fori_loop(1, everyone, scal_recv, 0)
    sums = scal[...].sum(axis=0)
    theta = jnp.sum(sums[0:1], keepdims=True) / jnp.sum(sums[1:2], keepdims=True)
    for t in range(nsec):
        resid_out[t] = (sig[t] - theta * w_ref[t, mine, :].astype(jnp.float32)).astype(jnp.bfloat16)
    lax.fori_loop(1, everyone, scal_sent, 0)


def local(n, n_op, wavefunction, left_ops, right_ops, energy, term_class, target_sector):
    terms, nsec, block, _ = left_ops.shape
    target_sector = target_sector.T
    rows = block // n_op
    vmem = pl.BlockSpec(memory_space=pltpu.VMEM)
    hbm = pl.BlockSpec(memory_space=pl.ANY)
    out = jax.ShapeDtypeStruct((nsec, rows, block), jnp.bfloat16)
    f32 = jnp.float32
    piece = (nsec, rows, block)
    pairs = []
    for count in ((nsec, 2), (nsec,), (nsec, PARTS), (nsec,), (nsec, PARTS)):
        pairs += [pltpu.SemaphoreType.DMA(count), pltpu.SemaphoreType.DMA(count)]
    return pl.pallas_call(
        functools.partial(kernel, n, n_op),
        out_shape=(out, out),
        in_specs=[hbm] * 6,
        out_specs=(vmem, vmem),
        scratch_shapes=[
            pltpu.SMEM((terms,), jnp.int32),
            pltpu.SMEM(target_sector.shape, jnp.int32),
            pltpu.SMEM((nsec,), f32),
            pltpu.VMEM((nsec, block, block), jnp.bfloat16),
            pltpu.VMEM((nsec, terms, block, block), jnp.bfloat16),
            pltpu.VMEM((nsec, terms, block, block), jnp.bfloat16),
            pltpu.VMEM((nsec, n_op, 5, rows, block), f32),
            pltpu.VMEM((nsec, 5, rows, block), f32),
            pltpu.VMEM((nsec, 5, rows, block), f32),
            pltpu.VMEM(piece, f32),
            pltpu.VMEM(piece, f32),
            pltpu.VMEM(piece, f32),
            pltpu.VMEM(piece, f32),
            pltpu.VMEM(piece, f32),
            pltpu.VMEM(piece, f32),
            pltpu.VMEM((n * n_op, 2, 128), f32),
            pltpu.SemaphoreType.DMA((4,)),
            pltpu.SemaphoreType.DMA((nsec, terms // GROUP)),
            pltpu.SemaphoreType.DMA((nsec, terms // GROUP)),
            *pairs,
            pltpu.SemaphoreType.DMA((n * n_op,)),
            pltpu.SemaphoreType.DMA((n * n_op,)),
        ],
        compiler_params=pltpu.CompilerParams(
            collective_id=0, has_side_effects=True, vmem_limit_bytes=60 * 1024 * 1024
        ),
        cost_estimate=pl.CostEstimate(
            flops=4 * terms * nsec * block**3, bytes_accessed=4 * terms * nsec * block**2, transcendentals=0
        ),
    )(term_class, target_sector, energy, wavefunction, left_ops, right_ops)


def solution(mesh):
    in_specs = (
        P(("groups", "sector"), None, None),
        P("op", ("groups", "sector"), None, None),
        P("op", ("groups", "sector"), None, None),
        P(("groups", "sector")),
        P("op"),
        P("groups", None),
    )
    out_specs = (P(("groups", "sector"), "op", None), P(("groups", "sector"), "op", None))
    body = functools.partial(local, mesh.shape["sector"], mesh.shape["op"])
    return jax.shard_map(body, mesh=mesh, in_specs=in_specs, out_specs=out_specs, check_vma=False)
```

time: 41.7 us -> 42.9 us (1.029)
  Pallas kernels: 36.4 us -> 38.9 us
  local copies, waits for them, and re-layouts: 4.43 us -> 3.23 us
    pallas_call x1, Pallas kernels: 36.4 us -> 38.9 us  [local(): pl.pallas_call(functools.partial(kernel, n, n_op), out_shape=(out, out),...]
    unnamed x9 -> x2, local copies, waits for them, and re-layouts: 4.43 us -> 3.23 us
where the time goes in v2:
time: 42.9 us; the launch traced here: 42.7 us
  Pallas kernels  38.9 us (91%)
  local copies, waits for them, and re-layouts  3.23 us (8%)
  between operations  0.64 us (1%)
    pallas_call x1, Pallas kernels, local(): pl.pallas_call(functools.partial(kernel, n, n_op), out_shape=(out, out),...  38.9 us
    unnamed x2, local copies, waits for them, and re-layouts  3.23 us

profile of v2, /device:TPU:0, one launch (start us, length us, event | category | flops | bytes accessed | tf_op | source)
XLA Modules:
  0.0 42.7 jit_solution(10394273543661292143)
XLA Ops:
  0.6 38.9 %shard_map.77 = (bf16[3,128,256]{2,1,0:T(8,128)(2,1)}, bf16[3,128,256]{2,1,0:T(8,128)(2,1)}) custom-call(s32[16]{0:T(128)} %tc_in.1, s32[5,24]{1,0:T(8,128)} %bitcast.1, f32[3]{0:T(128)} %energy_in.1, bf16[3,256,256]{2,1,0:T(8,128)(2,1)} %w_in.1, bf16[16,3,256,256]{3,2,1,0:T(8,128)(2,1)} %left.1, bf16[16,3,256,256]{3,2,1,0:T(8,128)(2,1)} %right.1), custom_call_target="tpu_custom_call" | custom-call | flops 3221225472 | bytes 12582912 | tf_op jit(solution)/shard_map/pallas_call | solution.py:254
  39.5 1.6 %copy.10 = bf16[3,128,256]{2,1,0:T(8,128)(2,1)} copy(bf16[3,128,256]{2,1,0:T(8,128)(2,1)} %get-tuple-element.4) | data formatting | bytes 393216
  41.1 1.6 %copy.11 = bf16[3,128,256]{2,1,0:T(8,128)(2,1)} copy(bf16[3,128,256]{2,1,0:T(8,128)(2,1)} %get-tuple-element.5) | data formatting | bytes 393216

commit v3 on v2

--- a/solution.py
+++ b/solution.py
@@ -8,7 +8,7 @@
 from jax.sharding import PartitionSpec as P
 
 MESH = pl.DeviceIdType.MESH
-GROUP = 4
+GROUP = 8
 ALONE, VIA_PEER, TO_PEER, JOINED, OWN = range(5)
 FIRST = 2
 PARTS = 2
@@ -102,7 +102,7 @@
                 total = chosen[r][0] * products[0][h * rows:(h + 1) * rows]
                 for i in range(1, GROUP):
                     total = total + chosen[r][i] * products[i][h * rows:(h + 1) * rows]
-                acc[s, h, r] = total if g == 0 else acc[s, h, r] + total
+                acc[s, h, r] = acc[s, h, r] + total
 
     def finish_first(s):
         sib_copy(s, 0).wait_recv()
@@ -127,12 +127,19 @@
     for copy in smalls:
         copy.wait()
     for s in range(nsec):
-        for g in range(groups):
+        acc[s] = jnp.zeros(acc.shape[1:], jnp.float32)
+        middle = groups // 2 if s > 0 else 0
+
+        def step(g, carry, s=s):
             compute(s, g)
-            if s > 0 and g == 0:
-                finish_first(s - 1)
-            if s > 0 and g == groups - 1:
-                finish_second(s - 1)
+            return carry
+
+        lax.fori_loop(0, middle, step, 0)
+        if s > 0:
+            finish_first(s - 1)
+        lax.fori_loop(middle, groups, step, 0)
+        if s > 0:
+            finish_second(s - 1)
         if s == 0:
             pl.semaphore_wait(barrier, everyone - 1)
         for b in range(2):

time: 42.9 us -> 39.3 us (0.916)
  Pallas kernels: 38.9 us -> 35.2 us
    pallas_call x1, Pallas kernels: 38.9 us -> 35.2 us  [local(): pl.pallas_call(functools.partial(kernel, n, n_op), out_shape=(out, out),...]
where the time goes in v3:
time: 39.3 us; the launch traced here: 39.1 us
  Pallas kernels  35.2 us (90%)
  local copies, waits for them, and re-layouts  3.23 us (8%)
  between operations  0.64 us (2%)
    pallas_call x1, Pallas kernels, local(): pl.pallas_call(functools.partial(kernel, n, n_op), out_shape=(out, out),...  35.2 us
    unnamed x2, local copies, waits for them, and re-layouts  3.23 us

profile of v3, /device:TPU:0, one launch (start us, length us, event | category | flops | bytes accessed | tf_op | source)
XLA Modules:
  0.0 39.1 jit_solution(4793829706642678239)
XLA Ops:
  0.6 35.2 %shard_map.77 = (bf16[3,128,256]{2,1,0:T(8,128)(2,1)}, bf16[3,128,256]{2,1,0:T(8,128)(2,1)}) custom-call(s32[16]{0:T(128)} %tc_in.1, s32[5,24]{1,0:T(8,128)} %bitcast.1, f32[3]{0:T(128)} %energy_in.1, bf16[3,256,256]{2,1,0:T(8,128)(2,1)} %w_in.1, bf16[16,3,256,256]{3,2,1,0:T(8,128)(2,1)} %left.1, bf16[16,3,256,256]{3,2,1,0:T(8,128)(2,1)} %right.1), custom_call_target="tpu_custom_call" | custom-call | flops 3221225472 | bytes 12582912 | tf_op jit(solution)/shard_map/pallas_call | solution.py:261
  35.9 1.6 %copy.10 = bf16[3,128,256]{2,1,0:T(8,128)(2,1)} copy(bf16[3,128,256]{2,1,0:T(8,128)(2,1)} %get-tuple-element.4) | data formatting | bytes 393216
  37.5 1.6 %copy.11 = bf16[3,128,256]{2,1,0:T(8,128)(2,1)} copy(bf16[3,128,256]{2,1,0:T(8,128)(2,1)} %get-tuple-element.5) | data formatting | bytes 393216

commit v4 on v3

--- a/solution.py
+++ b/solution.py
@@ -120,9 +120,6 @@
         sib_copy(s, 1).wait_recv()
         for r in (TO_PEER, JOINED, OWN):
             tot[s, r] = acc[s, core, r] + sib[s, r]
-        if s == nsec - 1:
-            for q in range(nsec):
-                peer_copy(q).start()
 
     for copy in smalls:
         copy.wait()
@@ -165,6 +162,9 @@
                 total = total + own_w[t][j] * tot[j, JOINED, part] + via_w[t][j] * via_in[j, part]
             joined[t, part] = total
             joined_copy(t, p).start()
+        for q in range(nsec):
+            if min(q, PARTS - 1) == p:
+                peer_copy(q).start()
 
     mine = pl.ds(pl.multiple_of(core * rows, rows), rows)
     norm = jnp.zeros((8, block), jnp.float32)

time: 39.3 us -> 39.3 us (level)
  no operation moved by 1% of the time
where the time goes in v4:
time: 39.3 us; the launch traced here: 39.1 us
  Pallas kernels  35.2 us (90%)
  local copies, waits for them, and re-layouts  3.23 us (8%)
  between operations  0.64 us (2%)
    pallas_call x1, Pallas kernels, local(): pl.pallas_call(functools.partial(kernel, n, n_op), out_shape=(out, out),...  35.2 us
    unnamed x2, local copies, waits for them, and re-layouts  3.23 us

profile of v4, /device:TPU:0, one launch (start us, length us, event | category | flops | bytes accessed | tf_op | source)
XLA Modules:
  0.0 39.1 jit_solution(15550456786343443907)
XLA Ops:
  0.6 35.2 %shard_map.77 = (bf16[3,128,256]{2,1,0:T(8,128)(2,1)}, bf16[3,128,256]{2,1,0:T(8,128)(2,1)}) custom-call(s32[16]{0:T(128)} %tc_in.1, s32[5,24]{1,0:T(8,128)} %bitcast.1, f32[3]{0:T(128)} %energy_in.1, bf16[3,256,256]{2,1,0:T(8,128)(2,1)} %w_in.1, bf16[16,3,256,256]{3,2,1,0:T(8,128)(2,1)} %left.1, bf16[16,3,256,256]{3,2,1,0:T(8,128)(2,1)} %right.1), custom_call_target="tpu_custom_call" | custom-call | flops 3221225472 | bytes 12582912 | tf_op jit(solution)/shard_map/pallas_call | solution.py:261
  35.9 1.6 %copy.10 = bf16[3,128,256]{2,1,0:T(8,128)(2,1)} copy(bf16[3,128,256]{2,1,0:T(8,128)(2,1)} %get-tuple-element.4) | data formatting | bytes 393216
  37.5 1.6 %copy.11 = bf16[3,128,256]{2,1,0:T(8,128)(2,1)} copy(bf16[3,128,256]{2,1,0:T(8,128)(2,1)} %get-tuple-element.5) | data formatting | bytes 393216
